TPU v7x, 256 devices: a whole 4x4x8 slice. The times are simulated.
256 devices in a mesh: samp: 32 (over x, z), blk: 8 (over y, core).
Axes of the slice: x: 4, y: 4, z: 8, core: 2. Of those that a mesh axis runs over, the one named last changes fastest.
Arguments:
- genotypes: bfloat16 [262144, 4096], P('samp', 'blk'), may hold values from -20 to 20
- phenotypes: bfloat16 [4, 262144], P(None, 'samp'), may hold values from -8 to 8
Outputs:
- predicted: float32 [4, 262144], P(None, ('samp', 'blk'))
- coefficients: float32 [20, 4096], P(None, 'blk')
All inputs are finite; a program needn't handle non-finite values.
Results may differ from a plain program's by a relative error of at most 0.0013.
Values may be sent and summed in bfloat16 or wider, within the bound.
A program may use at most 64 MiB of HBM per device.

v0:
```python
import jax
import jax.numpy as jnp
from jax import lax
from jax.sharding import PartitionSpec as P

TRAIT_COUNT = 4
PENALTY_COUNT = 5


ridge_levels = (0.1, 0.4, 1.6, 6.4, 25.6)
level_penalty = 0.5


def solve_level_one(second_level_gram, second_level_cross, count_of_blocks):
    item_count = count_of_blocks * PENALTY_COUNT
    reshaped_array = second_level_gram.reshape(
        count_of_blocks, TRAIT_COUNT, PENALTY_COUNT, count_of_blocks, TRAIT_COUNT, PENALTY_COUNT
    )
    diag_part = jnp.diagonal(reshaped_array, axis1=1, axis2=4)
    systems = jnp.transpose(diag_part, (4, 0, 1, 2, 3)).reshape(TRAIT_COUNT, item_count, item_count)
    systems = systems + level_penalty * jnp.eye(item_count, dtype=jnp.float32)[None]
    partial_cross = jnp.diagonal(
        second_level_cross.reshape(count_of_blocks, TRAIT_COUNT, PENALTY_COUNT, TRAIT_COUNT),
        axis1=1,
        axis2=3,
    )
    right_side = jnp.transpose(partial_cross, (2, 0, 1)).reshape(TRAIT_COUNT, item_count, 1)
    cholesky_factor = jnp.linalg.cholesky(systems)
    ridge_weights = jax.scipy.linalg.cho_solve((cholesky_factor, True), right_side)
    return ridge_weights.reshape(TRAIT_COUNT, count_of_blocks, PENALTY_COUNT)


def inner_rows(left_side, right_side):
    return lax.dot_general(
        left_side, right_side, (((0,), (0,)), ((), ())), preferred_element_type=jnp.float32
    )


def outer_cols(left_side, right_side):
    return lax.dot_general(
        left_side, right_side, (((1,), (1,)), ((), ())), preferred_element_type=jnp.float32
    )


def local(genotypes, phenotypes):
    sample_rows = genotypes.shape[0]
    width_of_block = genotypes.shape[1]
    sample_total = sample_rows * lax.axis_size("samp")
    count_of_blocks = lax.axis_size("blk")
    partial_cross = lax.dot_general(
        genotypes, phenotypes, (((0,), (1,)), ((), ())), preferred_element_type=jnp.float32
    )
    gram_part = inner_rows(genotypes, genotypes)
    gram_matrix, cross_product_matrix = lax.psum((gram_part, partial_cross), "samp")
    gram_matrix = gram_matrix / sample_total
    cross_product_matrix = cross_product_matrix / sample_total
    penalty_values = jnp.array(ridge_levels, dtype=jnp.float32)
    identity_matrix = jnp.eye(width_of_block, dtype=jnp.float32)
    systems = gram_matrix[None] + penalty_values[:, None, None] * identity_matrix[None]
    cholesky_factor = jnp.linalg.cholesky(systems)
    solved_system = jax.scipy.linalg.cho_solve(
        (cholesky_factor, True),
        jnp.broadcast_to(cross_product_matrix, (PENALTY_COUNT, width_of_block, TRAIT_COUNT)),
    )
    coefficients = jnp.transpose(solved_system, (2, 0, 1)).reshape(
        TRAIT_COUNT * PENALTY_COUNT, width_of_block
    )
    preds = outer_cols(coefficients.astype(jnp.bfloat16), genotypes).astype(jnp.bfloat16)
    sample_portion = sample_rows // count_of_blocks
    offset = lax.axis_index("blk") * sample_portion
    every_prediction = lax.all_gather(preds, "blk", axis=0, tiled=True)
    second_level_gram, second_level_cross = lax.psum(
        (outer_cols(every_prediction, every_prediction), outer_cols(every_prediction, phenotypes)),
        "samp",
    )
    local_predictions = lax.dynamic_slice_in_dim(every_prediction, offset, sample_portion, 1)
    ridge_weights = solve_level_one(
        second_level_gram / sample_total, second_level_cross / sample_total, count_of_blocks
    )
    reshaped_predictions = local_predictions.reshape(
        count_of_blocks, TRAIT_COUNT, PENALTY_COUNT, sample_portion
    ).astype(jnp.float32)
    predicted = jnp.einsum(
        "tbk,btks->ts", ridge_weights, reshaped_predictions, precision=lax.Precision.HIGHEST
    )
    return (predicted, coefficients)


def solution(mesh):
    placed = (P("samp", "blk"), P(None, "samp"))
    return jax.shard_map(
        local,
        mesh=mesh,
        in_specs=placed,
        out_specs=(P(None, ("samp", "blk")), P(None, "blk")),
        check_vma=False,
    )
```

profile of v0, /device:TPU:8, one launch (start us, length us, event | category | flops | bytes accessed | tf_op | source)
XLA Modules:
  0.0 1050.3 jit_solution(14191086175598590211)
XLA Ops:
  7.2 11.3 %fusion.63 = f32[512,512]{1,0:T(8,128)} fusion(bf16[8192,512]{1,0:T(8,128)(2,1)} %param.3), kind=kOutput, calls=%fused_computation.122 | convolution fusion | flops 4294967296 | bytes 9437184 | tf_op jit(solution)/shard_map/dot_general | solution.py:34
  18.6 4.6 fusion.64
  23.2 79.4 %psum.29 = f32[512,4]{0,1:T(4,128)S(1)} all-reduce(f32[512,4]{0,1:T(4,128)S(1)} %fusion.64), channel_id=1, replica_groups=mesh['samp'=32,'blk'=8] {'samp'}, use_global_device_ids=true, to_apply=%region_9.10 | all-reduce | flops 2048 | bytes 16384 | tf_op jit(solution)/shard_map/psum | solution.py:54
  103.1 68.1 %all-reduce.4.cloned.1.call-done = f32[512,512]{1,0:T(8,128)} async-done(((f32[512,512]{1,0:T(8,128)}), f32[512,512]{1,0:T(8,128)}) %all-reduce.4.cloned.1.call-update) | async-done | bytes 1048592 | tf_op jit(solution)/shard_map/psum | solution.py:54
  180.9 58.6 %custom-call.49 = f32[5,128,128]{2,1,0:T(8,128)S(1)} custom-call(f32[5,128,128]{2,1,0:T(8,128)S(1)} %cholesky.312), custom_call_target="Cholesky" | custom-call | tf_op jit(solution)/shard_map/jit(cholesky)/cholesky | solution.py:60
  239.6 49.1 %custom-call.50 = f32[5,1,128,128]{2,3,1,0:T(8,128)S(1)} custom-call(f32[5,1,128,128]{3,2,1,0:T(8,128)S(1)} %select_bitcast_fusion.2), custom_call_target="InvertDiagBlocksLowerTriangular" | custom-call | tf_op jit(solution)/shard_map/jit(cholesky)/cholesky | solution.py:60
  297.2 58.8 %custom-call.51 = f32[5,128,128]{2,1,0:T(8,128)S(1)} custom-call(f32[5,128,128]{2,1,0:T(8,128)S(1)} %cholesky.316), custom_call_target="Cholesky" | custom-call | tf_op jit(solution)/shard_map/jit(cholesky)/cholesky | solution.py:60
  356.8 49.1 %custom-call.52 = f32[5,1,128,128]{2,3,1,0:T(8,128)S(1)} custom-call(f32[5,1,128,128]{3,2,1,0:T(8,128)S(1)} %get-tuple-element.29), custom_call_target="InvertDiagBlocksLowerTriangular" | custom-call | tf_op jit(solution)/shard_map/jit(cholesky)/cholesky | solution.py:60
  410.7 58.6 %custom-call.53 = f32[5,128,128]{2,1,0:T(8,128)S(1)} custom-call(f32[5,128,128]{2,1,0:T(8,128)S(1)} %cholesky.321), custom_call_target="Cholesky" | custom-call | tf_op jit(solution)/shard_map/jit(cholesky)/cholesky | solution.py:60
  470.1 49.3 %custom-call.54 = f32[5,1,128,128]{2,3,1,0:T(8,128)S(1)} custom-call(f32[5,1,128,128]{3,2,1,0:T(8,128)S(1)} %get-tuple-element.27), custom_call_target="InvertDiagBlocksLowerTriangular" | custom-call | tf_op jit(solution)/shard_map/jit(cholesky)/cholesky | solution.py:60
  523.8 58.6 %custom-call.55 = f32[5,128,128]{2,1,0:T(8,128)S(1)} custom-call(f32[5,128,128]{2,1,0:T(8,128)S(1)} %convolution_subtract_fusion.1), custom_call_target="Cholesky" | custom-call | tf_op jit(solution)/shard_map/jit(cholesky)/cholesky | solution.py:60
  583.8 5.7 select_select_fusion
  589.5 15.5 %while.1 = (s32[]{:T(128)}, f32[5,512,512]{2,1,0:T(8,128)}, s32[4,2]{0,1:T(2,128)S(1)}, f32[4,5,128,128]{3,2,0,1:T(8,128)}, s32[]{:T(128)}) while((s32[]{:T(128)}, f32[5,512,512]{2,1,0:T(8,128)}, s32[4,2]{0,1:T(2,128)S(1)}, f32[4,5,128,128]{3,2,0,1:T(8,128)}, s32[]{:T(128)}) %tuple.35), condition=%wide.while_cond, body=%wide.while_body.sunk | while | flops 2 | bytes 656993 | solution.py:61
  594.0 3.3 bitcast_dynamic-update-slice_fusion.2
  598.0 3.3 bitcast_dynamic-update-slice_fusion.2
  605.0 197.7 %custom-call.56 = f32[5,4,128,128]{2,3,1,0:T(8,128)S(1)} custom-call(f32[5,4,128,128]{3,2,1,0:T(8,128)} %bitcast.122), custom_call_target="InvertDiagBlocksLowerTriangular" | custom-call | tf_op jit(solution)/shard_map/jit(_cho_solve)/vmap()/triangular_solve | solution.py:61
  817.5 6.4 fusion
  825.4 25.5 %all-gather.3.cloned.1.call-done = bf16[8,20,8192]{2,1,0:T(8,128)(2,1)} async-done(((bf16[1,20,8192]{2,1,0:T(8,128)(2,1)}), bf16[8,20,8192]{2,1,0:T(8,128)(2,1)}) %all-gather.3.cloned.1.call-update) | async-done | bytes 2621456 | tf_op jit(solution)/shard_map/all_gather | solution.py:71
  856.1 75.1 %psum.31 = f32[160,4]{0,1:T(4,128)S(1)} all-reduce(f32[160,4]{0,1:T(4,128)S(1)} %fusion.66), channel_id=1, replica_groups=mesh['samp'=32,'blk'=8] {'samp'}, use_global_device_ids=true, to_apply=%region_13.14 | all-reduce | flops 640 | bytes 5120 | tf_op jit(solution)/shard_map/psum | solution.py:72
  932.1 67.6 %all-reduce.6.cloned.1.call-done = f32[160,160]{1,0:T(8,128)} async-done(((f32[160,160]{1,0:T(8,128)}), f32[160,160]{1,0:T(8,128)}) %all-reduce.6.cloned.1.call-update) | async-done | bytes 102416 | tf_op jit(solution)/shard_map/psum | solution.py:72
  1000.6 3.4 reshape.132
  1004.1 7.1 copy.86
  1014.6 14.7 %custom-call.57 = f32[4,40,40]{2,1,0:T(8,128)S(1)} custom-call(f32[4,40,40]{2,1,0:T(8,128)S(1)} %fusion.37), custom_call_target="Cholesky" | custom-call | tf_op jit(solution)/shard_map/jit(cholesky)/cholesky | solution.py:28
  1029.5 12.3 %custom-call.58 = f32[4,1,40,40]{2,3,1,0:T(8,128)S(1)} custom-call(f32[4,1,40,40]{3,2,1,0:T(8,128)S(1)} %select_bitcast_fusion.3), custom_call_target="InvertDiagBlocksLowerTriangular" | custom-call | tf_op jit(solution)/shard_map/jit(_cho_solve)/vmap()/triangular_solve | solution.py:29
  (106 shorter events, 68.3 us)
Async XLA Ops:
  7.2 11.5 %copy-start = (bf16[4,8192]{1,0:T(4,128)(2,1)S(1)}, bf16[4,8192]{1,0:T(4,128)(2,1)}, u32[]{:S(2)}) copy-start(bf16[4,8192]{1,0:T(4,128)(2,1)} %param.4) | copy-start | bytes 196612
  7.2 164.0 %all-reduce.4.cloned.1.call-start = ((), (), s32[]{:S(2)}) async-start(), calls=%async_computation | async-start | bytes 2097152 | tf_op jit(solution)/shard_map/psum | solution.py:54
  18.6 832.3 %all-gather.3.cloned.1.call-start = ((), (), s32[]{:S(2)}) async-start(), calls=%async_computation.2 | async-start | bytes 3538944 | tf_op jit(solution)/shard_map/all_gather | solution.py:71
  23.2 153.1 %copy-start.5 = (f32[5]{0:T(128)S(1)}, f32[5]{0:T(128)}, u32[]{:S(2)}) copy-start(f32[5]{0:T(128)} %constant.253.clone) | copy-start | bytes 64
  178.6 2.3 copy-start.1
  817.5 6.5 copy-start.2
  824.0 175.7 %all-reduce.6.cloned.1.call-start = ((), (), s32[]{:S(2)}) async-start(), calls=%async_computation.1 | async-start | bytes 327680 | tf_op jit(solution)/shard_map/psum | solution.py:72
  1000.6 13.9 %copy-start.3 = (f32[40,40]{0,1:T(8,128)S(1)}, f32[40,40]{0,1:T(8,128)}, u32[]{:S(2)}) copy-start(f32[40,40]{0,1:T(8,128)} %copy.88) | copy-start | bytes 19204
  1004.1 25.4 %copy-start.4 = (pred[40,40]{1,0:T(8,128)(4,1)S(1)}, pred[40,40]{1,0:T(8,128)(4,1)}, u32[]{:S(2)}) copy-start(pred[40,40]{1,0:T(8,128)(4,1)} %iota_compare_fusion.6) | copy-start | bytes 4804
Sparse Core Ops, SparseCore 0:
  18.7 152.4 all-reduce.3
  824.1 26.6 all-gather.2
  856.2 143.4 all-reduce.5
where the time goes:
time: 1050 us
  other arithmetic  623 us (59%)
  waiting for transfers between devices  161 us (15%)
  blocking collectives  155 us (15%)
  matrix products  54.8 us (5%)
  local copies, waits for them, and re-layouts  42.7 us (4%)
  between operations  14.3 us (1%)
    another operation x18, other arithmetic, local(): cholesky_factor = jnp.linalg.cholesky(systems)  385 us
    another operation x4, other arithmetic, local(): jax.scipy.linalg.cho_solve((cholesky_factor, True), jnp.broadcast_to(cros...  203 us
    psum x1, blocking collectives, local(): lax.psum((gram_part, partial_cross), 'samp')  79.4 us
    psum x1, blocking collectives, local(): lax.psum((outer_cols(every_prediction, every_prediction), outer_cols(ever...  75.1 us
    psum x1, waiting for transfers between devices, local(): lax.psum((gram_part, partial_cross), 'samp')  68.1 us
    psum x1, waiting for transfers between devices, local(): lax.psum((outer_cols(every_prediction, every_prediction), outer_cols(ever...  67.6 us
    all_gather x1, waiting for transfers between devices, local(): every_prediction = lax.all_gather(preds, 'blk', axis=0, tiled=True)  25.5 us
  transfers between devices with their start and end apart: 3, of which 3 were waited for; matrix products, arithmetic and copies ran while one was open for 1% of the time, Pallas kernels for 0%

commit v1 on v0

v1 whole, which is shorter than its diff:
```python
import jax
import jax.numpy as jnp
from jax import lax
from jax.experimental import pallas as pl
from jax.experimental.pallas import tpu as pltpu
from jax.sharding import PartitionSpec as P

TRAITS = 4
PENALTIES = 5
SAMPLES = 262144
BLOCK = 512
XS, ZS, BLKS = 4, 8, 8
ridge_levels = (0.1, 0.4, 1.6, 6.4, 25.6)
level_penalty = 0.5

ROWS = SAMPLES // (XS * ZS)
PART = ROWS // BLKS
F32 = jnp.float32
BF16 = jnp.bfloat16
HI = lax.Precision.HIGHEST
NT = (((1,), (1,)), ((), ()))
NN = (((1,), (0,)), ((), ()))
MESH = pl.DeviceIdType.MESH
VMEM = pltpu.VMEM

CHUNK = 2048
A_ROWS = 1024
B_ROWS = 512
PACKED = A_ROWS + B_ROWS


def place():
    samp = lax.axis_index("samp")
    return lax.div(samp, ZS), lax.rem(samp, ZS)


def along_x(x, z, step):
    other = lax.rem(x + step, XS)
    return other, {"samp": other * ZS + z}


def along_z(x, z, step):
    other = lax.rem(z + step, ZS)
    return other, {"samp": x * ZS + other}


def rows_at(index, size):
    return pl.ds(pl.multiple_of(index * size, size), size)


def send(src, dst, sems, slot, device):
    copy = pltpu.make_async_remote_copy(
        src_ref=src, dst_ref=dst, send_sem=sems.at[0, slot], recv_sem=sems.at[1, slot],
        device_id=device, device_id_type=MESH)
    copy.start()
    return copy


def finish(copies):
    for copy in copies:
        copy.wait()


def gram_sum_kernel(x_hbm, ph_ref, out_ref, xbuf, left, right, acc, ax, axs, az, azs, bz, bzs, bx, bxs,
                    load_sem, axr, azr, bzr, bxr, axg, azg, bzg, bxg):
    x, z = place()
    chunks = ROWS // CHUNK
    for c in range(chunks):
        pltpu.make_async_copy(x_hbm.at[pl.ds(c * CHUNK, CHUNK)], xbuf.at[pl.ds(c * CHUNK, CHUNK)], load_sem.at[c]).start()
    barrier = pltpu.get_barrier_semaphore()
    for step in range(1, XS):
        pl.semaphore_signal(barrier, inc=1, device_id=along_x(x, z, step)[1], device_id_type=MESH)
    for step in range(1, ZS):
        pl.semaphore_signal(barrier, inc=1, device_id=along_z(x, z, step)[1], device_id_type=MESH)

    left[...] = jnp.zeros_like(left)
    right[...] = jnp.zeros_like(right)
    for c in range(chunks):
        span = pl.ds(c * CHUNK, CHUNK)
        pltpu.make_async_copy(x_hbm.at[span], xbuf.at[span], load_sem.at[c]).wait()
        values = xbuf[span, :]
        flipped = jnp.concatenate([values.T, ph_ref[:, span], jnp.zeros((12, CHUNK), BF16)], 0)
        left[...] += lax.dot_general(flipped, values[:, :256], NN, preferred_element_type=F32)
        right[...] += lax.dot_general(flipped[256:], values[:, 256:], NN, preferred_element_type=F32)

    acc[0:512, :] = left[0:512, 0:128]
    acc[512:896, :] = left[128:512, 128:256]
    acc[896:1152, :] = right[0:256, 0:128]
    acc[1152:1280, :] = right[128:256, 128:256]
    acc[1280:1288, :] = jnp.concatenate([left[512:516, 0:128], left[512:516, 128:256]], 0)
    acc[1288:1296, :] = jnp.concatenate([right[256:260, 0:128], right[256:260, 128:256]], 0)
    acc[1296:PACKED, :] = jnp.zeros((PACKED - 1296, 128), F32)

    pl.semaphore_wait(barrier, XS - 1 + ZS - 1)
    a_out, b_out = [], []
    for step in range(1, ZS):
        other, device = along_z(x, z, step)
        src = acc.at[pl.ds(pl.multiple_of(A_ROWS + other * 64, 64), 64)]
        b_out.append(send(src, bz.at[step - 1], bzr, step - 1, device))
    for step in range(1, XS):
        other, device = along_x(x, z, step)
        a_out.append(send(acc.at[rows_at(other, 256)], ax.at[step - 1], axr, step - 1, device))
    finish(b_out)
    total = acc[pl.ds(pl.multiple_of(A_ROWS + z * 64, 64), 64), :]
    for i in range(ZS - 1):
        total = total + bz[i]
    bzs[...] = total
    b_out = []
    for step in range(1, XS):
        other, device = along_x(x, z, step)
        b_out.append(send(bzs.at[rows_at(other, 16)], bx.at[step - 1], bxr, step - 1, device))
    finish(a_out)
    total = acc[rows_at(x, 256), :]
    for i in range(XS - 1):
        total = total + ax[i]
    axs[...] = total
    a_out = []
    for step in range(1, ZS):
        other, device = along_z(x, z, step)
        a_out.append(send(axs.at[rows_at(other, 32)], az.at[step - 1], azr, step - 1, device))
    finish(b_out)
    total = bzs[rows_at(x, 16), :]
    for i in range(XS - 1):
        total = total + bx[i]
    bxs[rows_at(x, 16), :] = total
    b_out = []
    for step in range(1, XS):
        _, device = along_x(x, z, step)
        b_out.append(send(bxs.at[rows_at(x, 16)], bxs.at[rows_at(x, 16)], bxg, step - 1, device))
    finish(a_out)
    total = axs[rows_at(z, 32), :]
    for i in range(ZS - 1):
        total = total + az[i]
    azs[rows_at(z, 32), :] = total
    a_out = []
    for step in range(1, ZS):
        _, device = along_z(x, z, step)
        a_out.append(send(azs.at[rows_at(z, 32)], azs.at[rows_at(z, 32)], azg, step - 1, device))
    finish(b_out)
    out_ref[pl.ds(pl.multiple_of(A_ROWS + z * 64, 64), 64), :] = bxs[...]
    b_out = []
    for step in range(1, ZS):
        _, device = along_z(x, z, step)
        span = pl.ds(pl.multiple_of(A_ROWS + z * 64, 64), 64)
        b_out.append(send(bxs, out_ref.at[span], bzg, step - 1, device))
    finish(a_out)
    out_ref[rows_at(x, 256), :] = azs[...]
    a_out = []
    for step in range(1, XS):
        _, device = along_x(x, z, step)
        a_out.append(send(azs, out_ref.at[rows_at(x, 256)], axg, step - 1, device))
    finish(b_out)
    finish(a_out)


def dma(n):
    return pltpu.SemaphoreType.DMA((2, n))


def gram_sum(genotypes, phenotypes):
    x1, z1 = XS - 1, ZS - 1
    return pl.pallas_call(
        gram_sum_kernel,
        out_shape=jax.ShapeDtypeStruct((PACKED, 128), F32),
        in_specs=[pl.BlockSpec(memory_space=pl.ANY), pl.BlockSpec(memory_space=VMEM)],
        out_specs=pl.BlockSpec(memory_space=VMEM),
        scratch_shapes=[
            VMEM((ROWS, BLOCK), BF16), VMEM((528, 256), F32), VMEM((272, 256), F32), VMEM((PACKED, 128), F32),
            VMEM((x1, 256, 128), F32), VMEM((256, 128), F32), VMEM((z1, 32, 128), F32), VMEM((256, 128), F32),
            VMEM((z1, 64, 128), F32), VMEM((64, 128), F32), VMEM((x1, 16, 128), F32), VMEM((64, 128), F32),
            pltpu.SemaphoreType.DMA((ROWS // CHUNK,)),
            dma(x1), dma(z1), dma(z1), dma(x1), dma(x1), dma(z1), dma(z1), dma(x1),
        ],
        compiler_params=pltpu.CompilerParams(
            collective_id=0, has_side_effects=True, vmem_limit_bytes=40 << 20),
        name="gram_sum",
    )(genotypes, phenotypes)


def recip(d):
    r = pl.reciprocal(d, approx=True)
    r = r * (2.0 - d * r)
    r = r * (2.0 - d * r)
    return r


def tree(terms):
    while len(terms) > 1:
        terms = [terms[i] + terms[i + 1] for i in range(0, len(terms), 2)]
    return terms[0]


def sweep(rows, t, lane, sub):
    lo = 8 * t
    inside = (lane >= lo) & (lane < lo + 8)
    pivot_rows = rows[t]
    cols = [jnp.broadcast_to(pivot_rows[:, lo + j:lo + j + 1], (8, 128)) for j in range(8)]
    kept = jnp.where(inside, jnp.where(lane == sub + lo, 1.0, 0.0), pivot_rows)
    for p in range(8):
        col = cols[p]
        row = [jnp.broadcast_to(cols[j][p:p + 1, :], (8, 128)) for j in range(8)]
        r = recip(row[p])
        cols = [
            jnp.where(sub == p, r, -col * r) if j == p
            else jnp.where(sub == p, row[j] * r, cols[j] - (col * row[j]) * r)
            for j in range(8)
        ]
    new = tree([cols[j] * jnp.broadcast_to(kept[j:j + 1, :], (8, 128)) for j in range(8)])
    spread = [jnp.broadcast_to(new[j:j + 1, :], (8, 128)) for j in range(8)]
    out = []
    for i, group in enumerate(rows):
        if i == t:
            out.append(new)
        else:
            q = [jnp.broadcast_to(group[:, lo + j:lo + j + 1], (8, 128)) for j in range(8)]
            out.append(jnp.where(inside, 0.0, group) - tree([q[j] * spread[j] for j in range(8)]))
    return out


def iotas():
    shape = (8, 128)
    return lax.broadcasted_iota(jnp.int32, shape, 1), lax.broadcasted_iota(jnp.int32, shape, 0)


def solve0_kernel(g_ref, x_ref, a_ref, w_ref, inv_ref):
    lane, sub = iotas()
    _, z = place()
    which = lax.rem(z, PENALTIES)
    penalty = jnp.float32(ridge_levels[0])
    for k in range(1, PENALTIES):
        penalty = jnp.where(which == k, jnp.float32(ridge_levels[k]), penalty)
    base = (0, 512, 896, 1152)
    off = (0, 520, 912, 1176)
    for k in range(4):
        n = 512 - 128 * k
        a_ref[off[k]:off[k] + n, :] = g_ref[base[k]:base[k] + n, :] / SAMPLES
        cross = g_ref[1280 + 4 * k:1284 + 4 * k, :] / SAMPLES
        a_ref[off[k] + n:off[k] + n + 8, :] = jnp.concatenate([cross, jnp.zeros((4, 128), F32)], 0)
    for k in range(4):
        n = 512 - 128 * k
        rows = [a_ref[off[k] + 8 * i:off[k] + 8 * i + 8, :] + jnp.where(lane == sub + 8 * i, penalty, 0.0)
                for i in range(16)]
        for t in range(16):
            rows = sweep(rows, t, lane, sub)
        for i in range(16):
            inv_ref[8 * i:8 * i + 8, :] = rows[i]
        panel = a_ref[off[k] + 128:off[k] + n + 8, :]
        w = lax.dot_general(panel, inv_ref[...], NN, precision=HI, preferred_element_type=F32)
        w_ref[off[k]:off[k] + n - 120, :] = w
        for j in range(k + 1, 4):
            skip = 128 * (j - k - 1)
            change = lax.dot_general(panel[skip:, :], w[skip:skip + 128, :], NT, precision=HI, preferred_element_type=F32)
            a_ref[off[j]:off[j] + 520 - 128 * j, :] -= change
    parts = [None] * 4
    for k in (3, 2, 1, 0):
        n = 512 - 128 * k
        y = w_ref[off[k] + n - 128:off[k] + n - 120, :]
        if k < 3:
            later = jnp.concatenate(parts[k + 1:], 1)
            y = y - lax.dot_general(later, w_ref[off[k]:off[k] + n - 128, :], NN, precision=HI, preferred_element_type=F32)
        parts[k] = y
    x_ref[...] = jnp.concatenate(parts, 1)


def solve0(sums):
    return pl.pallas_call(
        solve0_kernel,
        out_shape=jax.ShapeDtypeStruct((8, BLOCK), F32),
        in_specs=[pl.BlockSpec(memory_space=VMEM)],
        out_specs=pl.BlockSpec(memory_space=VMEM),
        scratch_shapes=[VMEM((1312, 128), F32), VMEM((1312, 128), F32), VMEM((128, 128), F32)],
        name="solve0",
    )(sums)


def level1_kernel(beta_ref, ph_ref, x_hbm, pred_ref, coef_ref, xbuf, betas, low, stage, pall, lg, ly, lc, lx, lz, ls, wt, wts,
                  load_sem, bsem, psem, ysem, csem, xsem, zsem, wsem):
    x, z = place()
    blk = lax.axis_index("blk")
    y, core = lax.div(blk, 2), lax.rem(blk, 2)
    lane, sub = iotas()
    for c in range(BLKS):
        pltpu.make_async_copy(x_hbm.at[pl.ds(c * PART, PART)], xbuf.at[pl.ds(c * PART, PART)], load_sem.at[c]).start()
    barrier = pltpu.get_barrier_semaphore()
    for step in range(1, XS):
        pl.semaphore_signal(barrier, inc=1, device_id=along_x(x, z, step)[1], device_id_type=MESH)
    for step in range(1, ZS):
        pl.semaphore_signal(barrier, inc=1, device_id=along_z(x, z, step)[1], device_id_type=MESH)
    for step in range(1, BLKS):
        pl.semaphore_signal(barrier, inc=1, device_id={"blk": lax.rem(blk + step, BLKS)}, device_id_type=MESH)
    for c in range(BLKS):
        pltpu.make_async_copy(x_hbm.at[pl.ds(c * PART, PART)], xbuf.at[pl.ds(c * PART, PART)], load_sem.at[c]).wait()
    pl.semaphore_wait(barrier, XS + ZS + BLKS - 3)

    def to(k, other):
        return pltpu.make_async_remote_copy(
            src_ref=beta_ref, dst_ref=betas.at[k], send_sem=bsem.at[0, other], recv_sem=bsem.at[1, k],
            device_id={"samp": x * ZS + other}, device_id_type=MESH)

    for k in range(PENALTIES):
        @pl.when(z == k)
        def _():
            for step in range(1, ZS):
                to(k, (k + step) % ZS).start()
            betas[k] = beta_ref[...]
    for k in range(PENALTIES):
        @pl.when(z == k)
        def _():
            for step in range(1, ZS):
                to(k, (k + step) % ZS).wait_send()

        @pl.when(z != k)
        def _():
            to(k, 0).wait_recv()
    groups = []
    for t in range(TRAITS):
        groups.append(jnp.concatenate([betas[k][t:t + 1, :] for k in range(PENALTIES)], 0))
    coef_ref[...] = jnp.concatenate(groups, 0)
    blank = jnp.zeros((8 - PENALTIES, BLOCK), F32)
    low[...] = jnp.concatenate([v for g in groups for v in (g, blank)], 0).astype(BF16)

    def predict(owner):
        part = xbuf[rows_at(owner, PART), :]
        return lax.dot_general(low[...], part, NT, preferred_element_type=F32).astype(BF16)

    def part_copy(step):
        owner = lax.rem(blk + step, BLKS)
        return pltpu.make_async_remote_copy(
            src_ref=stage.at[step], dst_ref=pall.at[blk], send_sem=psem.at[0, step], recv_sem=psem.at[1, step],
            device_id={"blk": owner}, device_id_type=MESH)

    def emit(step, carry):
        stage[step] = predict(lax.rem(blk + step, BLKS))
        part_copy(step).start()
        return carry

    lax.fori_loop(1, BLKS, emit, 0)
    pall[blk] = predict(blk)

    def landed(step, carry):
        part_copy(step).wait()
        return carry

    lax.fori_loop(1, BLKS, landed, 0)

    preds = pall[...].astype(F32)
    own = ph_ref[:, rows_at(blk, PART)]
    tail = jnp.concatenate([own, jnp.zeros((12, PART), BF16)], 0)
    by_trait = []
    for t in range(TRAITS):
        pt = preds[:, 8 * t:8 * t + 8, :].reshape(64, PART).astype(BF16)
        by_trait.append(pt)
        sums = lax.dot_general(jnp.concatenate([pt, tail], 0), pt, NT, preferred_element_type=F32)
        lg[t, 0:32, :] = jnp.concatenate([sums[0:32], sums[32:64]], 1)
        lg[t, 32:40, :] = jnp.concatenate([sums[64:72], jnp.zeros((8, 64), F32)], 1)
    copies = []
    for step in range(1, 4):
        other = lax.rem(y + step, 4)
        copies.append(send(lg.at[other], ly.at[step - 1], ysem, step - 1, {"blk": other * 2 + core}))
    finish(copies)
    total = lg[y]
    for i in range(3):
        total = total + ly[i]
    ls[0] = total
    finish([send(ls.at[0], lc, csem, 0, {"blk": y * 2 + 1 - core})])
    ls[1] = total + lc[...]
    copies = []
    for step in range(1, XS):
        copies.append(send(ls.at[1], lx.at[step - 1], xsem, step - 1, along_x(x, z, step)[1]))
    finish(copies)
    total = ls[1]
    for i in range(XS - 1):
        total = total + lx[i]
    ls[2] = total
    copies = []
    for step in range(1, ZS):
        copies.append(send(ls.at[2], lz.at[step - 1], zsem, step - 1, along_z(x, z, step)[1]))
    finish(copies)
    total = ls[2]
    for i in range(ZS - 1):
        total = total + lz[i]
    total = total / SAMPLES
    blank = jnp.zeros((32, 64), F32)
    full = jnp.concatenate([
        jnp.concatenate([total[0:32, 0:64], blank], 1),
        jnp.concatenate([total[0:32, 64:128], blank], 1),
        total[32:40]], 0)
    rows = [full[8 * i:8 * i + 8] + (jnp.where(lane == sub + 8 * i, level_penalty, 0.0) if i < 8 else 0.0) for i in range(9)]
    for t in range(8):
        rows = sweep(rows, t, lane, sub)
    mine = jnp.where(sub == y, -rows[8], 0.0)
    wt[...] = mine
    copies = []
    for step in range(1, 4):
        other = lax.rem(y + step, 4)
        copies.append(send(wt, wts.at[step - 1], wsem, step - 1, {"blk": other * 2 + core}))
    finish(copies)
    weights = mine + wts[0] + wts[1] + wts[2]
    wide = jnp.concatenate([jnp.where(sub == t, weights, 0.0)[:, 0:64] for t in range(TRAITS)], 1)
    w1 = wide.astype(BF16).astype(F32)
    w2 = (wide - w1).astype(BF16).astype(F32)
    w3 = wide - w1 - w2
    parts = jnp.concatenate([w1, w2, w3, jnp.zeros((8, 256), F32)], 0).astype(BF16)
    terms = lax.dot_general(parts, jnp.concatenate(by_trait, 0), NN, preferred_element_type=F32)
    pred_ref[...] = (terms[0:8] + terms[8:16] + terms[16:24])[0:4]


def level1(beta, phenotypes, genotypes):
    return pl.pallas_call(
        level1_kernel,
        out_shape=(jax.ShapeDtypeStruct((TRAITS, PART), F32), jax.ShapeDtypeStruct((TRAITS * PENALTIES, BLOCK), F32)),
        in_specs=[pl.BlockSpec(memory_space=VMEM), pl.BlockSpec(memory_space=VMEM), pl.BlockSpec(memory_space=pl.ANY)],
        out_specs=(pl.BlockSpec(memory_space=VMEM),) * 2,
        scratch_shapes=[
            VMEM((ROWS, BLOCK), BF16), VMEM((PENALTIES, 8, BLOCK), F32), VMEM((32, BLOCK), BF16),
            VMEM((BLKS, 32, PART), BF16), VMEM((BLKS, 32, PART), BF16),
            VMEM((4, 40, 128), F32), VMEM((3, 40, 128), F32), VMEM((40, 128), F32), VMEM((XS - 1, 40, 128), F32),
            VMEM((ZS - 1, 40, 128), F32), VMEM((3, 40, 128), F32), VMEM((8, 128), F32), VMEM((3, 8, 128), F32),
            pltpu.SemaphoreType.DMA((BLKS,)),
            dma(ZS), dma(BLKS), dma(3), dma(1), dma(XS - 1), dma(ZS - 1), dma(3),
        ],
        compiler_params=pltpu.CompilerParams(
            collective_id=1, has_side_effects=True, vmem_limit_bytes=40 << 20),
        name="level1",
    )(beta, phenotypes, genotypes)


def local(genotypes, phenotypes):
    sums = gram_sum(genotypes, phenotypes)
    beta = solve0(sums)
    return level1(beta, phenotypes, genotypes)


def solution(mesh):
    return jax.shard_map(
        local,
        mesh=mesh,
        in_specs=(P("samp", "blk"), P(None, "samp")),
        out_specs=(P(None, ("samp", "blk")), P(None, "blk")),
        check_vma=False,
    )
```

time: 1050 us -> 115 us (0.11)
  other arithmetic: 623 us -> 0 us
  waiting for transfers between devices: 161 us -> 0 us
  blocking collectives: 155 us -> 0 us
  Pallas kernels: 0 us -> 103 us
  matrix products: 54.8 us -> 0 us
  local copies, waits for them, and re-layouts: 42.7 us -> 10.4 us
  between operations: 14.3 us -> 0.67 us
    another operation x29 -> x0, other arithmetic: 617 us -> none  [the longest x18 385 us: local(): cholesky_factor = jnp.linalg.cholesky(systems)]
    psum x2 -> x0, blocking collectives: 155 us -> none  [the longest x1 79.4 us: local(): lax.psum((gram_part, partial_cross), 'samp')]
    psum x2 -> x0, waiting for transfers between devices: 136 us -> none  [the longest x1 68.1 us: local(): lax.psum((gram_part, partial_cross), 'samp')]
    pallas_call x0 -> x3, Pallas kernels: none -> 103 us  [the longest x1 41.3 us: gram_sum(): pl.pallas_call(gram_sum_kernel, out_shape=jax.ShapeDtypeStruct((PACKED, 1...]
    another operation x22 -> x0, matrix products: 29.6 us -> none  [the longest x14 14.7 us: local(): jax.scipy.linalg.cho_solve((cholesky_factor, True), jnp.broadcast_to(cros...]
    all_gather x1 -> x0, waiting for transfers between devices: 25.5 us -> none  [local(): every_prediction = lax.all_gather(preds, 'blk', axis=0, tiled=True)]
    dot_general x6 -> x0, matrix products: 25.2 us -> none  [the longest x1 11.3 us: inner_rows(): lax.dot_general(left_side, right_side, (((0,), (0,)), ((), ())), preferre...]
    another operation x19 -> x0, local copies, waits for them, and re-layouts: 18.7 us -> none
  transfers between devices with their start and end apart: 3 -> 0, of which waited for: 3 -> 0; matrix products, arithmetic and copies ran while one was open for 1% -> 0% of each run, Pallas kernels for 0% -> 0%
where the time goes in v1:
time: 115 us; the launch traced here: 114 us
  Pallas kernels  103 us (90%)
  local copies, waits for them, and re-layouts  10.4 us (9%)
    pallas_call x1, Pallas kernels, gram_sum(): pl.pallas_call(gram_sum_kernel, out_shape=jax.ShapeDtypeStruct((PACKED, 1...  41.3 us
    pallas_call x1, Pallas kernels, level1(): pl.pallas_call(level1_kernel, out_shape=(jax.ShapeDtypeStruct((TRAITS, PA...  38.1 us
    pallas_call x1, Pallas kernels, solve0(): pl.pallas_call(solve0_kernel, out_shape=jax.ShapeDtypeStruct((8, BLOCK),...  23.5 us
    unnamed x14, local copies, waits for them, and re-layouts  10.4 us

profile of v1, /device:TPU:8, one launch (start us, length us, event | category | flops | bytes accessed | tf_op | source)
XLA Modules:
  0.0 114.0 jit_solution(6029612232127669515)
XLA Ops:
  0.6 0.0 copy-start
  0.6 3.4 %copy-done = bf16[8192,512]{1,0:T(8,128)(2,1)S(1)} copy-done((bf16[8192,512]{1,0:T(8,128)(2,1)S(1)}, bf16[8192,512]{1,0:T(8,128)(2,1)}, u32[]{:S(2)}) %copy-start) | copy-done | bytes 8388632
  4.0 0.0 copy-start.3
  4.0 0.8 copy-done.3
  4.9 0.0 copy-start.4
  4.9 41.3 %gram_sum.1.g_ref = f32[1536,128]{1,0:T(8,128)S(1)} custom-call(bf16[8192,512]{1,0:T(8,128)(2,1)S(1)} %copy-done, bf16[4,8192]{1,0:T(4,128)(2,1)S(1)} %copy-done.3), custom_call_target="tpu_custom_call" | custom-call | tf_op jit(solution)/shard_map/gram_sum/pallas_call | solution.py:162
  46.2 0.0 copy-start.2
  46.2 0.9 copy-done.2
  47.0 23.5 %solve0.1.beta_ref = f32[8,512]{1,0:T(8,128)} custom-call(f32[1536,128]{1,0:T(8,128)} %copy-done.2), custom_call_target="tpu_custom_call" | custom-call | tf_op jit(solution)/shard_map/solve0/pallas_call | solution.py:266
  70.5 0.0 copy-done.4
  70.5 0.0 copy-start.1
  70.5 3.4 %copy-done.1 = bf16[8192,512]{1,0:T(8,128)(2,1)S(1)} copy-done((bf16[8192,512]{1,0:T(8,128)(2,1)S(1)}, bf16[8192,512]{1,0:T(8,128)(2,1)}, u32[]{:S(2)}) %copy-start.1) | copy-done | bytes 8388632
  73.9 0.0 copy-start.5
  73.9 0.7 copy-done.5
  74.6 38.1 %level1.1 = (f32[4,1024]{1,0:T(4,128)S(1)}, f32[20,512]{1,0:T(8,128)S(1)}) custom-call(f32[8,512]{1,0:T(8,128)S(1)} %copy-done.5, bf16[4,8192]{1,0:T(4,128)(2,1)S(1)} %copy-done.4, bf16[8192,512]{1,0:T(8,128)(2,1)S(1)} %copy-done.1), custom_call_target="tpu_custom_call" | custom-call | tf_op jit(solution)/shard_map/level1/pallas_call | solution.py:409
  112.8 0.6 copy.6
  113.4 0.6 copy.7
Async XLA Ops:
  0.6 3.4 %copy-start = (bf16[8192,512]{1,0:T(8,128)(2,1)S(1)}, bf16[8192,512]{1,0:T(8,128)(2,1)}, u32[]{:S(2)}) copy-start(bf16[8192,512]{1,0:T(8,128)(2,1)} %x_hbm.3) | copy-start | bytes 25165828
  4.0 0.8 copy-start.3
  4.9 65.7 %copy-start.4 = (bf16[4,8192]{1,0:T(4,128)(2,1)S(1)}, bf16[4,8192]{1,0:T(4,128)(2,1)}, u32[]{:S(2)}) copy-start(bf16[4,8192]{1,0:T(4,128)(2,1)} %ph_ref.3) | copy-start | bytes 196612
  46.2 0.9 copy-start.2
  70.5 3.4 %copy-start.1 = (bf16[8192,512]{1,0:T(8,128)(2,1)S(1)}, bf16[8192,512]{1,0:T(8,128)(2,1)}, u32[]{:S(2)}) copy-start(bf16[8192,512]{1,0:T(8,128)(2,1)} %x_hbm.3) | copy-start | bytes 25165828
  73.9 0.7 copy-start.5

commit v2 on v1

v2 whole, which is shorter than its diff:
```python
import jax
import jax.numpy as jnp
from jax import lax
from jax.experimental import pallas as pl
from jax.experimental.pallas import tpu as pltpu
from jax.sharding import PartitionSpec as P

TRAITS = 4
PENALTIES = 5
SAMPLES = 262144
BLOCK = 512
XS, ZS, BLKS = 4, 8, 8
ridge_levels = (0.1, 0.4, 1.6, 6.4, 25.6)
level_penalty = 0.5

ROWS = SAMPLES // (XS * ZS)
PART = ROWS // BLKS
F32 = jnp.float32
BF16 = jnp.bfloat16
HI = lax.Precision.HIGHEST
NT = (((1,), (1,)), ((), ()))
NN = (((1,), (0,)), ((), ()))
MESH = pl.DeviceIdType.MESH
VMEM = pltpu.VMEM

CHUNK = 2048
A_ROWS = 1024
B_ROWS = 256
PACKED = A_ROWS + B_ROWS
OWNED = 40
USED = 1168
BELOW = {(1, 0): 0, (2, 0): 128, (3, 0): 256, (2, 1): 384, (3, 1): 512, (3, 2): 640}
TOP, CORNER, CROSS = 768, 1024, 1152

SOLVERS = ((0, 13), (9, 22), (18, 31), (27, 16), (4, 2))


def place():
    samp = lax.axis_index("samp")
    return lax.div(samp, ZS), lax.rem(samp, ZS)


def solver_of(k, core):
    first, second = SOLVERS[k]
    return first + core * (second - first)


def solves(samp, core):
    count = jnp.int32(0)
    for k in range(PENALTIES):
        count = count + jnp.where(samp == solver_of(k, core), jnp.int32(1), jnp.int32(0))
    return count


def along_x(x, z, step):
    other = lax.rem(x + step, XS)
    return other, {"samp": other * ZS + z}


def along_z(x, z, step):
    other = lax.rem(z + step, ZS)
    return other, {"samp": x * ZS + other}


def rows_at(index, size):
    return pl.ds(pl.multiple_of(index * size, size), size)


def send(src, dst, sems, slot, device):
    copy = pltpu.make_async_remote_copy(
        src_ref=src, dst_ref=dst, send_sem=sems.at[0, slot], recv_sem=sems.at[1, slot],
        device_id=device, device_id_type=MESH)
    copy.start()
    return copy


def finish(copies):
    for copy in copies:
        copy.wait()


def gram_sum_kernel(x_hbm, ph_ref, out_ref, xbuf, left, right, acc, ax, axs, az, bz, bzs, bx, mine,
                    load_sem, axr, azr, bzr, bxr, out_sem, in_sem):
    x, z = place()
    samp = lax.axis_index("samp")
    core = lax.rem(lax.axis_index("blk"), 2)
    chunks = ROWS // CHUNK
    for c in range(chunks):
        pltpu.make_async_copy(x_hbm.at[pl.ds(c * CHUNK, CHUNK)], xbuf.at[pl.ds(c * CHUNK, CHUNK)], load_sem.at[c]).start()
    barrier = pltpu.get_barrier_semaphore()
    for step in range(1, XS):
        pl.semaphore_signal(barrier, inc=1, device_id=along_x(x, z, step)[1], device_id_type=MESH)
    for step in range(1, ZS):
        pl.semaphore_signal(barrier, inc=1, device_id=along_z(x, z, step)[1], device_id_type=MESH)
    for k in range(PENALTIES):
        @pl.when(samp == solver_of(k, core))
        def _():
            def greet(step, carry):
                other = lax.rem(samp + step, XS * ZS)
                pl.semaphore_signal(barrier, inc=1, device_id={"samp": other}, device_id_type=MESH)
                return carry

            lax.fori_loop(1, XS * ZS, greet, 0)

    left[...] = jnp.zeros_like(left)
    right[...] = jnp.zeros_like(right)
    for c in range(chunks):
        span = pl.ds(c * CHUNK, CHUNK)
        pltpu.make_async_copy(x_hbm.at[span], xbuf.at[span], load_sem.at[c]).wait()
        values = xbuf[span, :]
        flipped = jnp.concatenate([values.T, ph_ref[:, span], jnp.zeros((12, CHUNK), BF16)], 0)
        left[...] += lax.dot_general(flipped, values[:, :256], NN, preferred_element_type=F32)
        right[...] += lax.dot_general(flipped[256:], values[:, 256:], NN, preferred_element_type=F32)

    def block(i, j, top=0, size=128):
        if j < 2:
            return left[128 * i + top:128 * i + top + size, 128 * j:128 * j + 128]
        return right[128 * i - 256 + top:128 * i - 256 + top + size, 128 * j - 256:128 * j - 128]

    for (i, j), row in BELOW.items():
        acc[row:row + 128, :] = block(i, j)
    for k in range(4):
        acc[TOP + 64 * k:TOP + 64 * k + 64, :] = block(k, k, 0, 64)
    for k in range(2):
        acc[CORNER + 64 * k:CORNER + 64 * k + 64, :] = jnp.concatenate(
            [block(2 * k, 2 * k, 64, 64)[:, 64:], block(2 * k + 1, 2 * k + 1, 64, 64)[:, 64:]], 1)
    acc[CROSS:CROSS + 8, :] = jnp.concatenate([left[512:516, 0:128], left[512:516, 128:256]], 0)
    acc[CROSS + 8:CROSS + 16, :] = jnp.concatenate([right[256:260, 0:128], right[256:260, 128:256]], 0)
    acc[USED:PACKED, :] = jnp.zeros((PACKED - USED, 128), F32)

    def b_rows(index):
        return pl.ds(pl.multiple_of(A_ROWS + index * 32, 32), 32)

    pl.semaphore_wait(barrier, XS + ZS - 2 + PENALTIES - solves(samp, core))
    a_out, b_out = [], []
    for step in range(1, ZS):
        other, device = along_z(x, z, step)
        b_out.append(send(acc.at[b_rows(other)], bz.at[step - 1], bzr, step - 1, device))
    for step in range(1, XS):
        other, device = along_x(x, z, step)
        a_out.append(send(acc.at[rows_at(other, 256)], ax.at[step - 1], axr, step - 1, device))
    finish(a_out)
    total = acc[rows_at(x, 256), :]
    for i in range(XS - 1):
        total = total + ax[i]
    axs[...] = total
    a_out = []
    for step in range(1, ZS):
        other, device = along_z(x, z, step)
        a_out.append(send(axs.at[rows_at(other, 32)], az.at[step - 1], azr, step - 1, device))
    finish(b_out)
    total = acc[b_rows(z), :]
    for i in range(ZS - 1):
        total = total + bz[i]
    bzs[...] = total
    b_out = []
    for step in range(1, XS):
        other, device = along_x(x, z, step)
        b_out.append(send(bzs.at[rows_at(other, 8)], bx.at[step - 1], bxr, step - 1, device))
    finish(b_out)
    total = bzs[rows_at(x, 8), :]
    for i in range(XS - 1):
        total = total + bx[i]
    mine[32:40, :] = total
    finish(a_out)
    total = axs[rows_at(z, 32), :]
    for i in range(ZS - 1):
        total = total + az[i]
    mine[0:32, :] = total

    def to(k, source):
        return pltpu.make_async_remote_copy(
            src_ref=mine, dst_ref=out_ref.at[rows_at(source, OWNED)], send_sem=out_sem.at[k], recv_sem=in_sem.at[source],
            device_id={"samp": solver_of(k, core)}, device_id_type=MESH)

    for k in range(PENALTIES):
        @pl.when(samp != solver_of(k, core))
        def _():
            to(k, samp).start()
    for k in range(PENALTIES):
        @pl.when(samp == solver_of(k, core))
        def _():
            out_ref[rows_at(samp, OWNED), :] = mine[...]

            def take(step, carry):
                to(k, lax.rem(samp + step, XS * ZS)).wait_recv()
                return carry

            lax.fori_loop(1, XS * ZS, take, 0)
    for k in range(PENALTIES):
        @pl.when(samp != solver_of(k, core))
        def _():
            to(k, samp).wait_send()


def dma(n):
    return pltpu.SemaphoreType.DMA((2, n))


def gram_sum(genotypes, phenotypes):
    x1, z1 = XS - 1, ZS - 1
    return pl.pallas_call(
        gram_sum_kernel,
        out_shape=jax.ShapeDtypeStruct((PACKED, 128), F32),
        in_specs=[pl.BlockSpec(memory_space=pl.ANY), pl.BlockSpec(memory_space=VMEM)],
        out_specs=pl.BlockSpec(memory_space=VMEM),
        scratch_shapes=[
            VMEM((ROWS, BLOCK), BF16), VMEM((528, 256), F32), VMEM((272, 256), F32), VMEM((PACKED, 128), F32),
            VMEM((x1, 256, 128), F32), VMEM((256, 128), F32), VMEM((z1, 32, 128), F32),
            VMEM((z1, 32, 128), F32), VMEM((32, 128), F32), VMEM((x1, 8, 128), F32), VMEM((OWNED, 128), F32),
            pltpu.SemaphoreType.DMA((ROWS // CHUNK,)),
            dma(x1), dma(z1), dma(z1), dma(x1), pltpu.SemaphoreType.DMA((PENALTIES,)), pltpu.SemaphoreType.DMA((XS * ZS,)),
        ],
        compiler_params=pltpu.CompilerParams(
            collective_id=0, has_side_effects=True, vmem_limit_bytes=57 << 20),
        name="gram_sum",
    )(genotypes, phenotypes)


def recip(d):
    r = pl.reciprocal(d, approx=True)
    r = r * (2.0 - d * r)
    r = r * (2.0 - d * r)
    return r


def tree(terms):
    while len(terms) > 1:
        terms = [terms[i] + terms[i + 1] for i in range(0, len(terms), 2)]
    return terms[0]


def sweep(rows, t, lane, sub):
    lo = 8 * t
    inside = (lane >= lo) & (lane < lo + 8)
    pivot_rows = rows[t]
    cols = [jnp.broadcast_to(pivot_rows[:, lo + j:lo + j + 1], (8, 128)) for j in range(8)]
    kept = jnp.where(inside, jnp.where(lane == sub + lo, 1.0, 0.0), pivot_rows)
    for p in range(8):
        col = cols[p]
        row = [jnp.broadcast_to(cols[j][p:p + 1, :], (8, 128)) for j in range(8)]
        r = recip(row[p])
        cols = [
            jnp.where(sub == p, r, -col * r) if j == p
            else jnp.where(sub == p, row[j] * r, cols[j] - (col * row[j]) * r)
            for j in range(8)
        ]
    new = tree([cols[j] * jnp.broadcast_to(kept[j:j + 1, :], (8, 128)) for j in range(8)])
    spread = [jnp.broadcast_to(new[j:j + 1, :], (8, 128)) for j in range(8)]
    out = []
    for i, group in enumerate(rows):
        if i == t:
            out.append(new)
        else:
            q = [jnp.broadcast_to(group[:, lo + j:lo + j + 1], (8, 128)) for j in range(8)]
            out.append(jnp.where(inside, 0.0, group) - tree([q[j] * spread[j] for j in range(8)]))
    return out


def iotas():
    shape = (8, 128)
    return lax.broadcasted_iota(jnp.int32, shape, 1), lax.broadcasted_iota(jnp.int32, shape, 0)


def solve0_kernel(g_ref, x_ref, a_ref, w_ref, inv_ref):
    lane, sub = iotas()
    samp = lax.axis_index("samp")
    core = lax.rem(lax.axis_index("blk"), 2)
    penalty = jnp.float32(ridge_levels[0])
    for k in range(1, PENALTIES):
        penalty = jnp.where(samp == solver_of(k, core), jnp.float32(ridge_levels[k]), penalty)

    def packed(row, count):
        pieces = []
        while count:
            if row < A_ROWS:
                owner, skip = row // 32, row % 32
                size = min(32 - skip, count)
                start = OWNED * owner + skip
            else:
                owner, skip = ((row - A_ROWS) % 32) // 8 * ZS + (row - A_ROWS) // 32, row % 8
                size = min(8 - skip, count)
                start = OWNED * owner + 32 + skip
            pieces.append(g_ref[start:start + size, :])
            row, count = row + size, count - size
        return (jnp.concatenate(pieces, 0) if len(pieces) > 1 else pieces[0]) / SAMPLES

    off = (0, 520, 912, 1176)
    for k in range(4):
        n = 512 - 128 * k
        upper = packed(TOP + 64 * k, 64)
        corner = packed(CORNER + 64 * (k // 2), 64)[:, 64 * (k % 2):64 * (k % 2) + 64]
        a_ref[off[k]:off[k] + 64, :] = upper
        a_ref[off[k] + 64:off[k] + 128, :] = jnp.concatenate([upper[:, 64:].T, corner], 1)
        for i in range(k + 1, 4):
            row = off[k] + 128 * (i - k)
            a_ref[row:row + 128, :] = packed(BELOW[i, k], 128)
        cross = packed(CROSS + 4 * k, 4)
        a_ref[off[k] + n:off[k] + n + 8, :] = jnp.concatenate([cross, jnp.zeros((4, 128), F32)], 0)
    for k in range(4):
        n = 512 - 128 * k
        rows = [a_ref[off[k] + 8 * i:off[k] + 8 * i + 8, :] + jnp.where(lane == sub + 8 * i, penalty, 0.0)
                for i in range(16)]
        for t in range(16):
            rows = sweep(rows, t, lane, sub)
        for i in range(16):
            inv_ref[8 * i:8 * i + 8, :] = rows[i]
        panel = a_ref[off[k] + 128:off[k] + n + 8, :]
        w = lax.dot_general(panel, inv_ref[...], NN, precision=HI, preferred_element_type=F32)
        w_ref[off[k]:off[k] + n - 120, :] = w
        for j in range(k + 1, 4):
            skip = 128 * (j - k - 1)
            change = lax.dot_general(panel[skip:, :], w[skip:skip + 128, :], NT, precision=HI, preferred_element_type=F32)
            a_ref[off[j]:off[j] + 520 - 128 * j, :] -= change
    parts = [None] * 4
    for k in (3, 2, 1, 0):
        n = 512 - 128 * k
        y = w_ref[off[k] + n - 128:off[k] + n - 120, :]
        if k < 3:
            later = jnp.concatenate(parts[k + 1:], 1)
            y = y - lax.dot_general(later, w_ref[off[k]:off[k] + n - 128, :], NN, precision=HI, preferred_element_type=F32)
        parts[k] = y
    x_ref[...] = jnp.concatenate([part[0:TRAITS] for part in parts], 0)


def solve0(sums):
    return pl.pallas_call(
        solve0_kernel,
        out_shape=jax.ShapeDtypeStruct((4 * TRAITS, 128), F32),
        in_specs=[pl.BlockSpec(memory_space=VMEM)],
        out_specs=pl.BlockSpec(memory_space=VMEM),
        scratch_shapes=[VMEM((1312, 128), F32), VMEM((1312, 128), F32), VMEM((128, 128), F32)],
        name="solve0",
    )(sums)


def level1_kernel(beta_ref, ph_ref, x_hbm, pred_ref, coef_ref, xbuf, betas, wide_low, stage, pall, lg, ly, lx, lz, ls, wt, wts,
                  load_sem, bsem, bget, psem, ysem, xsem, zsem, wsem):
    x, z = place()
    blk = lax.axis_index("blk")
    y, core = lax.div(blk, 2), lax.rem(blk, 2)
    lane, sub = iotas()
    for c in range(BLKS):
        pltpu.make_async_copy(x_hbm.at[pl.ds(c * PART, PART)], xbuf.at[pl.ds(c * PART, PART)], load_sem.at[c]).start()
    barrier = pltpu.get_barrier_semaphore()
    for step in range(1, XS):
        pl.semaphore_signal(barrier, inc=1, device_id=along_x(x, z, step)[1], device_id_type=MESH)
    for step in range(1, ZS):
        pl.semaphore_signal(barrier, inc=1, device_id=along_z(x, z, step)[1], device_id_type=MESH)
    for step in range(1, BLKS):
        pl.semaphore_signal(barrier, inc=1, device_id={"blk": lax.rem(blk + step, BLKS)}, device_id_type=MESH)
    samp = lax.axis_index("samp")
    for k in range(PENALTIES):
        @pl.when(samp != solver_of(k, core))
        def _():
            pl.semaphore_signal(barrier, inc=1, device_id={"samp": solver_of(k, core)}, device_id_type=MESH)
    pl.semaphore_wait(barrier, XS + ZS + BLKS - 3 + (XS * ZS - 1) * solves(samp, core))

    def to(k, step):
        other = lax.rem(solver_of(k, core) + step, XS * ZS)
        return pltpu.make_async_remote_copy(
            src_ref=beta_ref, dst_ref=betas.at[k], send_sem=bsem.at[step], recv_sem=bget.at[k],
            device_id={"samp": other}, device_id_type=MESH)

    for k in range(PENALTIES):
        @pl.when(samp == solver_of(k, core))
        def _():
            def start(step, carry):
                to(k, step).start()
                return carry

            lax.fori_loop(1, XS * ZS, start, 0)
            betas[k] = beta_ref[...]
    for c in range(BLKS):
        pltpu.make_async_copy(x_hbm.at[pl.ds(c * PART, PART)], xbuf.at[pl.ds(c * PART, PART)], load_sem.at[c]).wait()
    for k in range(PENALTIES):
        @pl.when(samp != solver_of(k, core))
        def _():
            to(k, 1).wait_recv()
    wide_low[...] = jnp.zeros_like(wide_low)
    for k in range(PENALTIES):
        for t in range(TRAITS):
            row = 4 * t + k if k < 4 else 16 + t
            for j in range(4):
                piece = betas[k, 4 * j + t:4 * j + t + 1, :]
                coef_ref[PENALTIES * t + k:PENALTIES * t + k + 1, 128 * j:128 * j + 128] = piece
                wide_low[row:row + 1, 128 * j:128 * j + 128] = piece
    low = wide_low[...].astype(BF16)

    quarter = PART // 4

    def predict(owner, dst):
        part = xbuf[rows_at(owner, PART), :]
        values = lax.dot_general(low, part, NT, preferred_element_type=F32)
        dst[:, 0:PART] = values[0:16].astype(BF16)
        last = values[16:20]
        dst[:, PART:] = jnp.concatenate([last[:, quarter * q:quarter * q + quarter] for q in range(4)], 0).astype(BF16)

    def part_copy(step):
        owner = lax.rem(blk + step, BLKS)
        return pltpu.make_async_remote_copy(
            src_ref=stage.at[step], dst_ref=pall.at[blk], send_sem=psem.at[0, step], recv_sem=psem.at[1, step],
            device_id={"blk": owner}, device_id_type=MESH)

    def emit(step, carry):
        predict(lax.rem(blk + step, BLKS), stage.at[step])
        part_copy(step).start()
        return carry

    lax.fori_loop(1, BLKS, emit, 0)
    predict(blk, pall.at[blk])

    def landed(step, carry):
        part_copy(step).wait()
        return carry

    lax.fori_loop(1, BLKS, landed, 0)

    for k in range(PENALTIES):
        @pl.when(samp == solver_of(k, core))
        def _():
            def sent(step, carry):
                to(k, step).wait_send()
                return carry

            lax.fori_loop(1, XS * ZS, sent, 0)

    own = ph_ref[:, rows_at(blk, PART)].astype(F32)
    mains = [pall[b, :, 0:PART].astype(F32) for b in range(BLKS)]
    lasts = [pall[b, :, PART:].astype(F32) for b in range(BLKS)]
    by_trait = []
    for t in range(TRAITS):
        fifth = [jnp.concatenate([last[4 * q + t:4 * q + t + 1] for last in lasts], 0) for q in range(4)]
        pt = jnp.concatenate([main[4 * t:4 * t + 4] for main in mains] + [jnp.concatenate(fifth, 1)], 0)
        rows = jnp.concatenate([pt, own, jnp.zeros((4, PART), F32)], 0).astype(BF16)
        pt = jnp.concatenate([pt, jnp.zeros((24, PART), F32)], 0).astype(BF16)
        by_trait.append(pt)
        sums = lax.dot_general(rows, pt, NT, preferred_element_type=F32)
        lg[t] = jnp.concatenate([sums[0:24], sums[24:48]], 1)
    copies = []
    for step in range(1, BLKS):
        other = lax.rem(blk + step, BLKS)
        copies.append(send(lg.at[lax.div(other, 2)], ly.at[step - 1], ysem, step - 1, {"blk": other}))
    finish(copies)
    total = lg[y]
    for i in range(BLKS - 1):
        total = total + ly[i]
    ls[1] = total
    copies = []
    for step in range(1, XS):
        copies.append(send(ls.at[1], lx.at[step - 1], xsem, step - 1, along_x(x, z, step)[1]))
    finish(copies)
    total = ls[1]
    for i in range(XS - 1):
        total = total + lx[i]
    ls[2] = total
    copies = []
    for step in range(1, ZS):
        copies.append(send(ls.at[2], lz.at[step - 1], zsem, step - 1, along_z(x, z, step)[1]))
    finish(copies)
    total = ls[2]
    for i in range(ZS - 1):
        total = total + lz[i]
    total = total / SAMPLES
    full = jnp.concatenate([total, jnp.concatenate([total[:, 64:128], jnp.zeros((24, 64), F32)], 1)], 0)
    full = jnp.where(lax.broadcasted_iota(jnp.int32, full.shape, 1) < 64, full, 0.0)
    rows = [full[8 * i:8 * i + 8] + (jnp.where(lane == sub + 8 * i, level_penalty, 0.0) if i < 5 else 0.0) for i in range(6)]
    for t in range(5):
        rows = sweep(rows, t, lane, sub)
    mine = jnp.where(sub == y, -rows[5], 0.0)
    wt[...] = mine
    copies = []
    for step in range(1, 4):
        other = lax.rem(y + step, 4)
        copies.append(send(wt, wts.at[step - 1], wsem, step - 1, {"blk": other * 2 + core}))
    finish(copies)
    weights = mine + wts[0] + wts[1] + wts[2]
    wide = jnp.concatenate([jnp.where(sub == t, weights, 0.0)[:, 0:64] for t in range(TRAITS)], 1)
    w1 = wide.astype(BF16).astype(F32)
    w2 = (wide - w1).astype(BF16).astype(F32)
    w3 = wide - w1 - w2
    parts = jnp.concatenate([w1, w2, w3, jnp.zeros((8, 256), F32)], 0).astype(BF16)
    terms = lax.dot_general(parts, jnp.concatenate(by_trait, 0), NN, preferred_element_type=F32)
    pred_ref[...] = (terms[0:8] + terms[8:16] + terms[16:24])[0:4]


def level1(beta, phenotypes, genotypes):
    return pl.pallas_call(
        level1_kernel,
        out_shape=(jax.ShapeDtypeStruct((TRAITS, PART), F32), jax.ShapeDtypeStruct((TRAITS * PENALTIES, BLOCK), F32)),
        in_specs=[pl.BlockSpec(memory_space=VMEM), pl.BlockSpec(memory_space=VMEM), pl.BlockSpec(memory_space=pl.ANY)],
        out_specs=(pl.BlockSpec(memory_space=VMEM),) * 2,
        scratch_shapes=[
            VMEM((ROWS, BLOCK), BF16), VMEM((PENALTIES, 4 * TRAITS, 128), F32), VMEM((32, BLOCK), F32),
            VMEM((BLKS, 16, PART + PART // 4), BF16), VMEM((BLKS, 16, PART + PART // 4), BF16),
            VMEM((4, 24, 128), F32), VMEM((BLKS - 1, 24, 128), F32), VMEM((XS - 1, 24, 128), F32),
            VMEM((ZS - 1, 24, 128), F32), VMEM((3, 24, 128), F32), VMEM((8, 128), F32), VMEM((3, 8, 128), F32),
            pltpu.SemaphoreType.DMA((BLKS,)),
            pltpu.SemaphoreType.DMA((XS * ZS,)), pltpu.SemaphoreType.DMA((PENALTIES,)), dma(BLKS), dma(BLKS - 1), dma(XS - 1), dma(ZS - 1), dma(3),
        ],
        compiler_params=pltpu.CompilerParams(
            collective_id=1, has_side_effects=True, vmem_limit_bytes=57 << 20),
        name="level1",
    )(beta, phenotypes, genotypes)


def local(genotypes, phenotypes):
    sums = gram_sum(genotypes, phenotypes)
    beta = solve0(sums)
    return level1(beta, phenotypes, genotypes)


def solution(mesh):
    return jax.shard_map(
        local,
        mesh=mesh,
        in_specs=(P("samp", "blk"), P(None, "samp")),
        out_specs=(P(None, ("samp", "blk")), P(None, "blk")),
        check_vma=False,
    )
```

time: 115 us -> 101 us (0.88)
  local copies, waits for them, and re-layouts: 10.4 us -> 2.74 us
  Pallas kernels: 103 us -> 97.5 us
    unnamed x14 -> x2, local copies, waits for them, and re-layouts: 10.4 us -> 2.74 us
    pallas_call x1, Pallas kernels: 41.3 us -> 34.6 us  [gram_sum(): pl.pallas_call(gram_sum_kernel, out_shape=jax.ShapeDtypeStruct((PACKED, 1...]
where the time goes in v2:
time: 101 us
  Pallas kernels  97.5 us (97%)
  local copies, waits for them, and re-layouts  2.74 us (3%)
    pallas_call x1, Pallas kernels, level1(): pl.pallas_call(level1_kernel, out_shape=(jax.ShapeDtypeStruct((TRAITS, PA...  39.2 us
    pallas_call x1, Pallas kernels, gram_sum(): pl.pallas_call(gram_sum_kernel, out_shape=jax.ShapeDtypeStruct((PACKED, 1...  34.6 us
    pallas_call x1, Pallas kernels, solve0(): pl.pallas_call(solve0_kernel, out_shape=jax.ShapeDtypeStruct((4 * TRAITS,...  23.7 us
    unnamed x2, local copies, waits for them, and re-layouts  2.74 us

profile of v2, /device:TPU:8, one launch (start us, length us, event | category | flops | bytes accessed | tf_op | source)
XLA Modules:
  0.0 100.9 jit_solution(3581587514122390857)
XLA Ops:
  0.6 34.6 %gram_sum.1.g_ref = f32[1280,128]{1,0:T(8,128)} custom-call(bf16[8192,512]{1,0:T(8,128)(2,1)} %x_hbm.3, bf16[4,8192]{1,0:T(4,128)(2,1)} %ph_ref.3), custom_call_target="tpu_custom_call" | custom-call | tf_op jit(solution)/shard_map/gram_sum/pallas_call | solution.py:202
  35.2 23.7 %solve0.1.beta_ref = f32[16,128]{1,0:T(8,128)} custom-call(f32[1280,128]{1,0:T(8,128)} %gram_sum.1.g_ref), custom_call_target="tpu_custom_call" | custom-call | tf_op jit(solution)/shard_map/solve0/pallas_call | solution.py:327
  59.0 39.2 %level1.1 = (f32[4,1024]{1,0:T(4,128)}, f32[20,512]{1,0:T(8,128)}) custom-call(f32[16,128]{1,0:T(8,128)} %solve0.1.beta_ref, bf16[4,8192]{1,0:T(4,128)(2,1)} %ph_ref.3, bf16[8192,512]{1,0:T(8,128)(2,1)} %x_hbm.3), custom_call_target="tpu_custom_call" | custom-call | tf_op jit(solution)/shard_map/level1/pallas_call | solution.py:488
  98.2 1.3 %copy.6 = f32[4,1024]{1,0:T(4,128)} copy(f32[4,1024]{1,0:T(4,128)} %get-tuple-element.4) | data formatting | bytes 32768
  99.5 1.4 %copy.7 = f32[20,512]{1,0:T(8,128)} copy(f32[20,512]{1,0:T(8,128)} %get-tuple-element.5) | data formatting | bytes 81920

commit v3 on v2

--- a/solution.py
+++ b/solution.py
@@ -79,7 +79,7 @@
         copy.wait()
 
 
-def gram_sum_kernel(x_hbm, ph_ref, out_ref, xbuf, left, right, acc, ax, axs, az, bz, bzs, bx, mine,
+def gram_sum(x_hbm, ph_ref, out_ref, xbuf, left, right, acc, ax, axs, az, bz, bzs, bx, mine,
                     load_sem, axr, azr, bzr, bxr, out_sem, in_sem):
     x, z = place()
     samp = lax.axis_index("samp")
@@ -102,6 +102,14 @@
 
             lax.fori_loop(1, XS * ZS, greet, 0)
 
+    for step in range(1, BLKS):
+        other = lax.rem(lax.axis_index("blk") + step, BLKS)
+        pl.semaphore_signal(barrier, inc=1, device_id={"blk": other}, device_id_type=MESH)
+    for k in range(PENALTIES):
+        @pl.when(samp != solver_of(k, core))
+        def _():
+            pl.semaphore_signal(barrier, inc=1, device_id={"samp": solver_of(k, core)}, device_id_type=MESH)
+
     left[...] = jnp.zeros_like(left)
     right[...] = jnp.zeros_like(right)
     for c in range(chunks):
@@ -131,7 +139,8 @@
     def b_rows(index):
         return pl.ds(pl.multiple_of(A_ROWS + index * 32, 32), 32)
 
-    pl.semaphore_wait(barrier, XS + ZS - 2 + PENALTIES - solves(samp, core))
+    solving = solves(samp, core)
+    pl.semaphore_wait(barrier, XS + ZS + BLKS - 3 + PENALTIES - solving + (XS * ZS - 1) * solving)
     a_out, b_out = [], []
     for step in range(1, ZS):
         other, device = along_z(x, z, step)
@@ -197,29 +206,8 @@
     return pltpu.SemaphoreType.DMA((2, n))
 
 
-def gram_sum(genotypes, phenotypes):
-    x1, z1 = XS - 1, ZS - 1
-    return pl.pallas_call(
-        gram_sum_kernel,
-        out_shape=jax.ShapeDtypeStruct((PACKED, 128), F32),
-        in_specs=[pl.BlockSpec(memory_space=pl.ANY), pl.BlockSpec(memory_space=VMEM)],
-        out_specs=pl.BlockSpec(memory_space=VMEM),
-        scratch_shapes=[
-            VMEM((ROWS, BLOCK), BF16), VMEM((528, 256), F32), VMEM((272, 256), F32), VMEM((PACKED, 128), F32),
-            VMEM((x1, 256, 128), F32), VMEM((256, 128), F32), VMEM((z1, 32, 128), F32),
-            VMEM((z1, 32, 128), F32), VMEM((32, 128), F32), VMEM((x1, 8, 128), F32), VMEM((OWNED, 128), F32),
-            pltpu.SemaphoreType.DMA((ROWS // CHUNK,)),
-            dma(x1), dma(z1), dma(z1), dma(x1), pltpu.SemaphoreType.DMA((PENALTIES,)), pltpu.SemaphoreType.DMA((XS * ZS,)),
-        ],
-        compiler_params=pltpu.CompilerParams(
-            collective_id=0, has_side_effects=True, vmem_limit_bytes=57 << 20),
-        name="gram_sum",
-    )(genotypes, phenotypes)
-
-
 def recip(d):
     r = pl.reciprocal(d, approx=True)
-    r = r * (2.0 - d * r)
     r = r * (2.0 - d * r)
     return r
 
@@ -262,7 +250,7 @@
     return lax.broadcasted_iota(jnp.int32, shape, 1), lax.broadcasted_iota(jnp.int32, shape, 0)
 
 
-def solve0_kernel(g_ref, x_ref, a_ref, w_ref, inv_ref):
+def solve0(g_ref, x_ref, a_ref, w_ref, inv_ref):
     lane, sub = iotas()
     samp = lax.axis_index("samp")
     core = lax.rem(lax.axis_index("blk"), 2)
@@ -323,39 +311,13 @@
     x_ref[...] = jnp.concatenate([part[0:TRAITS] for part in parts], 0)
 
 
-def solve0(sums):
-    return pl.pallas_call(
-        solve0_kernel,
-        out_shape=jax.ShapeDtypeStruct((4 * TRAITS, 128), F32),
-        in_specs=[pl.BlockSpec(memory_space=VMEM)],
-        out_specs=pl.BlockSpec(memory_space=VMEM),
-        scratch_shapes=[VMEM((1312, 128), F32), VMEM((1312, 128), F32), VMEM((128, 128), F32)],
-        name="solve0",
-    )(sums)
-
-
-def level1_kernel(beta_ref, ph_ref, x_hbm, pred_ref, coef_ref, xbuf, betas, wide_low, stage, pall, lg, ly, lx, lz, ls, wt, wts,
-                  load_sem, bsem, bget, psem, ysem, xsem, zsem, wsem):
+def level1(beta_ref, ph_ref, pred_ref, coef_ref, xbuf, betas, wide_low, stage, pall, lg, ly, lx, lz, ls, wt, wts,
+           bsem, bget, psem, ysem, xsem, zsem, wsem):
     x, z = place()
     blk = lax.axis_index("blk")
     y, core = lax.div(blk, 2), lax.rem(blk, 2)
     lane, sub = iotas()
-    for c in range(BLKS):
-        pltpu.make_async_copy(x_hbm.at[pl.ds(c * PART, PART)], xbuf.at[pl.ds(c * PART, PART)], load_sem.at[c]).start()
-    barrier = pltpu.get_barrier_semaphore()
-    for step in range(1, XS):
-        pl.semaphore_signal(barrier, inc=1, device_id=along_x(x, z, step)[1], device_id_type=MESH)
-    for step in range(1, ZS):
-        pl.semaphore_signal(barrier, inc=1, device_id=along_z(x, z, step)[1], device_id_type=MESH)
-    for step in range(1, BLKS):
-        pl.semaphore_signal(barrier, inc=1, device_id={"blk": lax.rem(blk + step, BLKS)}, device_id_type=MESH)
     samp = lax.axis_index("samp")
-    for k in range(PENALTIES):
-        @pl.when(samp != solver_of(k, core))
-        def _():
-            pl.semaphore_signal(barrier, inc=1, device_id={"samp": solver_of(k, core)}, device_id_type=MESH)
-    pl.semaphore_wait(barrier, XS + ZS + BLKS - 3 + (XS * ZS - 1) * solves(samp, core))
-
     def to(k, step):
         other = lax.rem(solver_of(k, core) + step, XS * ZS)
         return pltpu.make_async_remote_copy(
@@ -371,8 +333,6 @@
 
             lax.fori_loop(1, XS * ZS, start, 0)
             betas[k] = beta_ref[...]
-    for c in range(BLKS):
-        pltpu.make_async_copy(x_hbm.at[pl.ds(c * PART, PART)], xbuf.at[pl.ds(c * PART, PART)], load_sem.at[c]).wait()
     for k in range(PENALTIES):
         @pl.when(samp != solver_of(k, core))
         def _():
@@ -484,30 +444,48 @@
     pred_ref[...] = (terms[0:8] + terms[8:16] + terms[16:24])[0:4]
 
 
-def level1(beta, phenotypes, genotypes):
+def ridge_kernel(x_hbm, ph_ref, pred_ref, coef_ref, xbuf, sums, beta, *scratch):
+    samp = lax.axis_index("samp")
+    core = lax.rem(lax.axis_index("blk"), 2)
+    gram_sum(x_hbm, ph_ref, sums, xbuf, *scratch[:17])
+
+    @pl.when(solves(samp, core) == 1)
+    def _():
+        solve0(sums, beta, *scratch[17:20])
+
+    level1(beta, ph_ref, pred_ref, coef_ref, xbuf, *scratch[20:])
+
+
+def local(genotypes, phenotypes):
+    x1, z1 = XS - 1, ZS - 1
+    sems = pltpu.SemaphoreType.DMA
+    gram_scratch = [
+        VMEM((528, 256), F32), VMEM((272, 256), F32), VMEM((PACKED, 128), F32),
+        VMEM((x1, 256, 128), F32), VMEM((256, 128), F32), VMEM((z1, 32, 128), F32),
+        VMEM((z1, 32, 128), F32), VMEM((32, 128), F32), VMEM((x1, 8, 128), F32), VMEM((OWNED, 128), F32),
+        sems((ROWS // CHUNK,)), dma(x1), dma(z1), dma(z1), dma(x1), sems((PENALTIES,)), sems((XS * ZS,)),
+    ]
+    solve_scratch = [VMEM((1312, 128), F32), VMEM((1312, 128), F32), VMEM((128, 128), F32)]
+    level1_scratch = [
+        VMEM((PENALTIES, 4 * TRAITS, 128), F32), VMEM((32, BLOCK), F32),
+        VMEM((BLKS, 16, PART + PART // 4), BF16), VMEM((BLKS, 16, PART + PART // 4), BF16),
+        VMEM((4, 24, 128), F32), VMEM((BLKS - 1, 24, 128), F32), VMEM((x1, 24, 128), F32),
+        VMEM((z1, 24, 128), F32), VMEM((3, 24, 128), F32), VMEM((8, 128), F32), VMEM((3, 8, 128), F32),
+        sems((XS * ZS,)), sems((PENALTIES,)), dma(BLKS), dma(BLKS - 1), dma(x1), dma(z1), dma(3),
+    ]
     return pl.pallas_call(
-        level1_kernel,
+        ridge_kernel,
         out_shape=(jax.ShapeDtypeStruct((TRAITS, PART), F32), jax.ShapeDtypeStruct((TRAITS * PENALTIES, BLOCK), F32)),
-        in_specs=[pl.BlockSpec(memory_space=VMEM), pl.BlockSpec(memory_space=VMEM), pl.BlockSpec(memory_space=pl.ANY)],
+        in_specs=[pl.BlockSpec(memory_space=pl.ANY), pl.BlockSpec(memory_space=VMEM)],
         out_specs=(pl.BlockSpec(memory_space=VMEM),) * 2,
         scratch_shapes=[
-            VMEM((ROWS, BLOCK), BF16), VMEM((PENALTIES, 4 * TRAITS, 128), F32), VMEM((32, BLOCK), F32),
-            VMEM((BLKS, 16, PART + PART // 4), BF16), VMEM((BLKS, 16, PART + PART // 4), BF16),
-            VMEM((4, 24, 128), F32), VMEM((BLKS - 1, 24, 128), F32), VMEM((XS - 1, 24, 128), F32),
-            VMEM((ZS - 1, 24, 128), F32), VMEM((3, 24, 128), F32), VMEM((8, 128), F32), VMEM((3, 8, 128), F32),
-            pltpu.SemaphoreType.DMA((BLKS,)),
-            pltpu.SemaphoreType.DMA((XS * ZS,)), pltpu.SemaphoreType.DMA((PENALTIES,)), dma(BLKS), dma(BLKS - 1), dma(XS - 1), dma(ZS - 1), dma(3),
+            VMEM((ROWS, BLOCK), BF16), VMEM((XS * ZS * OWNED, 128), F32), VMEM((4 * TRAITS, 128), F32),
+            *gram_scratch, *solve_scratch, *level1_scratch,
         ],
         compiler_params=pltpu.CompilerParams(
-            collective_id=1, has_side_effects=True, vmem_limit_bytes=57 << 20),
-        name="level1",
-    )(beta, phenotypes, genotypes)
-
-
-def local(genotypes, phenotypes):
-    sums = gram_sum(genotypes, phenotypes)
-    beta = solve0(sums)
-    return level1(beta, phenotypes, genotypes)
+            collective_id=0, has_side_effects=True, vmem_limit_bytes=57 << 20),
+        name="ridge",
+    )(genotypes, phenotypes)
 
 
 def solution(mesh):

time: 101 us -> 90.9 us (0.900)
  Pallas kernels: 97.5 us -> 87.3 us
    pallas_call x3 -> x1, Pallas kernels: 97.5 us -> 87.3 us  [local(): pl.pallas_call(ridge_kernel, out_shape=(jax.ShapeDtypeStruct((TRAITS, PAR...]
where the time goes in v3:
time: 90.9 us; the launch traced here: 90.7 us
  Pallas kernels  87.3 us (96%)
  local copies, waits for them, and re-layouts  2.74 us (3%)
    pallas_call x1, Pallas kernels, local(): pl.pallas_call(ridge_kernel, out_shape=(jax.ShapeDtypeStruct((TRAITS, PAR...  87.3 us
    unnamed x2, local copies, waits for them, and re-layouts  2.74 us

profile of v3, /device:TPU:8, one launch (start us, length us, event | category | flops | bytes accessed | tf_op | source)
XLA Modules:
  0.0 90.7 jit_solution(9622467066643169834)
XLA Ops:
  0.6 87.3 %ridge.1 = (f32[4,1024]{1,0:T(4,128)}, f32[20,512]{1,0:T(8,128)}) custom-call(bf16[8192,512]{1,0:T(8,128)(2,1)} %x_hbm.1, bf16[4,8192]{1,0:T(4,128)(2,1)} %ph_ref.1), custom_call_target="tpu_custom_call" | custom-call | tf_op jit(solution)/shard_map/ridge/pallas_call | solution.py:476
  88.0 1.3 %copy.6 = f32[4,1024]{1,0:T(4,128)} copy(f32[4,1024]{1,0:T(4,128)} %get-tuple-element.4) | data formatting | bytes 32768
  89.3 1.4 %copy.7 = f32[20,512]{1,0:T(8,128)} copy(f32[20,512]{1,0:T(8,128)} %get-tuple-element.5) | data formatting | bytes 81920

commit v4 on v3

--- a/solution.py
+++ b/solution.py
@@ -28,6 +28,11 @@
 B_ROWS = 256
 PACKED = A_ROWS + B_ROWS
 OWNED = 40
+X_STEPS = (2, 1, 3)
+Z_STEPS = (4, 3, 5, 2, 6, 1, 7)
+FAR_FIRST = sorted(
+    ((dx, dz) for dx in range(XS) for dz in range(ZS) if dx or dz),
+    key=lambda step: -(min(step[0], XS - step[0]) + min(step[1], ZS - step[1])))
 USED = 1168
 BELOW = {(1, 0): 0, (2, 0): 128, (3, 0): 256, (2, 1): 384, (3, 1): 512, (3, 2): 640}
 TOP, CORNER, CROSS = 768, 1024, 1152
@@ -142,10 +147,10 @@
     solving = solves(samp, core)
     pl.semaphore_wait(barrier, XS + ZS + BLKS - 3 + PENALTIES - solving + (XS * ZS - 1) * solving)
     a_out, b_out = [], []
-    for step in range(1, ZS):
+    for step in Z_STEPS:
         other, device = along_z(x, z, step)
         b_out.append(send(acc.at[b_rows(other)], bz.at[step - 1], bzr, step - 1, device))
-    for step in range(1, XS):
+    for step in X_STEPS:
         other, device = along_x(x, z, step)
         a_out.append(send(acc.at[rows_at(other, 256)], ax.at[step - 1], axr, step - 1, device))
     finish(a_out)
@@ -154,7 +159,7 @@
         total = total + ax[i]
     axs[...] = total
     a_out = []
-    for step in range(1, ZS):
+    for step in Z_STEPS:
         other, device = along_z(x, z, step)
         a_out.append(send(axs.at[rows_at(other, 32)], az.at[step - 1], azr, step - 1, device))
     finish(b_out)
@@ -163,7 +168,7 @@
         total = total + bz[i]
     bzs[...] = total
     b_out = []
-    for step in range(1, XS):
+    for step in X_STEPS:
         other, device = along_x(x, z, step)
         b_out.append(send(bzs.at[rows_at(other, 8)], bx.at[step - 1], bxr, step - 1, device))
     finish(b_out)
@@ -318,25 +323,27 @@
     y, core = lax.div(blk, 2), lax.rem(blk, 2)
     lane, sub = iotas()
     samp = lax.axis_index("samp")
-    def to(k, step):
-        other = lax.rem(solver_of(k, core) + step, XS * ZS)
+    which = jnp.int32(0)
+    for k in range(1, PENALTIES):
+        which = which + jnp.where(samp == solver_of(k, core), jnp.int32(k), jnp.int32(0))
+    solving = solves(samp, core)
+
+    def to(k, dx, dz):
+        other = lax.rem(x + dx, XS) * ZS + lax.rem(z + dz, ZS)
         return pltpu.make_async_remote_copy(
-            src_ref=beta_ref, dst_ref=betas.at[k], send_sem=bsem.at[step], recv_sem=bget.at[k],
+            src_ref=beta_ref, dst_ref=betas.at[k], send_sem=bsem.at[dx * ZS + dz], recv_sem=bget.at[k],
             device_id={"samp": other}, device_id_type=MESH)
 
-    for k in range(PENALTIES):
-        @pl.when(samp == solver_of(k, core))
-        def _():
-            def start(step, carry):
-                to(k, step).start()
-                return carry
-
-            lax.fori_loop(1, XS * ZS, start, 0)
-            betas[k] = beta_ref[...]
+    @pl.when(solving == 1)
+    def _():
+        for dx, dz in FAR_FIRST:
+            to(which, dx, dz).start()
+        betas[which] = beta_ref[...]
+
     for k in range(PENALTIES):
         @pl.when(samp != solver_of(k, core))
         def _():
-            to(k, 1).wait_recv()
+            to(k, 0, 1).wait_recv()
     wide_low[...] = jnp.zeros_like(wide_low)
     for k in range(PENALTIES):
         for t in range(TRAITS):
@@ -376,14 +383,10 @@
 
     lax.fori_loop(1, BLKS, landed, 0)
 
-    for k in range(PENALTIES):
-        @pl.when(samp == solver_of(k, core))
-        def _():
-            def sent(step, carry):
-                to(k, step).wait_send()
-                return carry
-
-            lax.fori_loop(1, XS * ZS, sent, 0)
+    @pl.when(solving == 1)
+    def _():
+        for dx, dz in FAR_FIRST:
+            to(which, dx, dz).wait_send()
 
     own = ph_ref[:, rows_at(blk, PART)].astype(F32)
     mains = [pall[b, :, 0:PART].astype(F32) for b in range(BLKS)]
@@ -407,7 +410,7 @@
         total = total + ly[i]
     ls[1] = total
     copies = []
-    for step in range(1, XS):
+    for step in X_STEPS:
         copies.append(send(ls.at[1], lx.at[step - 1], xsem, step - 1, along_x(x, z, step)[1]))
     finish(copies)
     total = ls[1]
@@ -415,7 +418,7 @@
         total = total + lx[i]
     ls[2] = total
     copies = []
-    for step in range(1, ZS):
+    for step in Z_STEPS:
         copies.append(send(ls.at[2], lz.at[step - 1], zsem, step - 1, along_z(x, z, step)[1]))
     finish(copies)
     total = ls[2]
@@ -483,7 +486,7 @@
             *gram_scratch, *solve_scratch, *level1_scratch,
         ],
         compiler_params=pltpu.CompilerParams(
-            collective_id=0, has_side_effects=True, vmem_limit_bytes=57 << 20),
+            collective_id=0, has_side_effects=True, vmem_limit_bytes=50 << 20),
         name="ridge",
     )(genotypes, phenotypes)
 

time: 90.9 us -> 86.7 us (0.954)
  Pallas kernels: 87.3 us -> 83.8 us
    pallas_call x1, Pallas kernels: 87.3 us -> 83.8 us  [local(): pl.pallas_call(ridge_kernel, out_shape=(jax.ShapeDtypeStruct((TRAITS, PAR...]
    unnamed x2 -> x4, local copies, waits for them, and re-layouts: 2.74 us -> 2.06 us
where the time goes in v4:
time: 86.7 us; the launch traced here: 86.5 us
  Pallas kernels  83.8 us (97%)
  local copies, waits for them, and re-layouts  2.06 us (2%)
    pallas_call x1, Pallas kernels, local(): pl.pallas_call(ridge_kernel, out_shape=(jax.ShapeDtypeStruct((TRAITS, PAR...  83.8 us
    unnamed x4, local copies, waits for them, and re-layouts  2.06 us

profile of v4, /device:TPU:8, one launch (start us, length us, event | category | flops | bytes accessed | tf_op | source)
XLA Modules:
  0.0 86.5 jit_solution(17676992557543148561)
XLA Ops:
  0.6 0.0 copy-start
  0.6 0.8 copy-done
  1.5 83.8 %ridge.1 = (f32[4,1024]{1,0:T(4,128)S(1)}, f32[20,512]{1,0:T(8,128)S(1)}) custom-call(bf16[8192,512]{1,0:T(8,128)(2,1)} %x_hbm.1, bf16[4,8192]{1,0:T(4,128)(2,1)S(1)} %copy-done), custom_call_target="tpu_custom_call" | custom-call | tf_op jit(solution)/shard_map/ridge/pallas_call | solution.py:479
  85.3 0.6 copy.6
  85.9 0.6 copy.7
Async XLA Ops:
  0.6 0.8 copy-start
